TPU v7x, 512 devices: a whole 4x4x16 slice. The times are simulated.
512 devices in a mesh: pair: 128 (over y_hi, x, z), rep: 4 (over y_lo, core).
Axes of the slice: x: 4, y: 4 (y_hi: 2, y_lo: 2; y = y_hi * 2 + y_lo), z: 16, core: 2. Of those that a mesh axis runs over, the one named last changes fastest.
Arguments:
- amplitudes: bfloat16 [36864, 768], P('pair'), may hold values from -24 to 24
- lambda_amps: bfloat16 [36864, 4608], P('pair', 'rep'), may hold values from -6 to 6
- integrals: bfloat16 [768, 4608], P(None, 'rep'), may hold values from -0.21875 to 0.21875
- pair_map: int32 [384, 8], replicated, may hold values from 0 to 1, as said below
Outputs:
- ladder: bfloat16 [36864, 4608], P('pair', 'rep')
- lambda_ladder: bfloat16 [36864, 768], P('pair', 'rep')
- density: float32 [768, 4608], P('pair', 'rep')
Inputs may be any that keep to these rules, and one draw needn't show every extreme that they name: `pair_map`: 1 marks a live block of an occupied-pair tile and a window virtual-pair tile, 0 an empty one.
All inputs are finite; a program needn't handle non-finite values.
Results may differ from a plain program's by a relative error of at most 0.013.
Values may be sent and summed in bfloat16 or wider, within the bound.
A program may use at most 64 MiB of HBM per device.

v0:
```python
import jax
import jax.numpy as jnp
from jax import lax
from jax.sharding import PartitionSpec as P

TW = 96


def body(amplitudes, lambda_amps, integrals, pair_map):
    local_pairs = amplitudes.shape[0]
    tiles = pair_map.shape[0]
    pair_rows = lax.axis_index("pair") * local_pairs + jnp.arange(local_pairs, dtype=jnp.int32)
    owner_tile = pair_rows // TW
    selector = (owner_tile[:, None] == jnp.arange(tiles, dtype=jnp.int32)[None, :]).astype(
        jnp.float32
    )
    tile_mask = jnp.dot(selector, pair_map.astype(jnp.float32))
    live_mask = jnp.repeat(tile_mask, TW, axis=1)
    amp_live = amplitudes * live_mask.astype(jnp.bfloat16)
    factor = 1.0 / (local_pairs * lax.axis_size("pair")) ** 0.5
    ladder_sum = jnp.dot(amp_live, integrals, preferred_element_type=jnp.float32)
    partial_value = lax.dot_general(
        lambda_amps, integrals, (((1,), (1,)), ((), ())), preferred_element_type=jnp.float32
    )
    masked = partial_value * live_mask
    summed = lax.psum_scatter(masked.astype(jnp.bfloat16), "rep", scatter_dimension=1, tiled=True)
    ladder = ladder_sum.astype(jnp.bfloat16)
    density = lax.psum_scatter(
        lax.dot_general(
            amp_live, lambda_amps, (((0,), (0,)), ((), ())), preferred_element_type=jnp.float32
        )
        * factor,
        "pair",
        scatter_dimension=0,
        tiled=True,
    )
    return (ladder, summed, density)


def solution(mesh):
    in_specs = (P("pair", None), P("pair", "rep"), P(None, "rep"), P())
    out_specs = (P("pair", "rep"), P("pair", "rep"), P("pair", "rep"))
    return jax.shard_map(body, mesh=mesh, in_specs=in_specs, out_specs=out_specs, check_vma=False)
```

profile of v0, /device:TPU:24, one launch (start us, length us, event | category | flops | bytes accessed | tf_op | source)
XLA Modules:
  0.0 1393.4 jit_solution(16835069084968604553)
XLA Ops:
  8.0 0.0 copy-start
  8.0 0.0 reduce-scatter.4.cloned.1.call-start
  8.1 0.0 copy-start.1
  8.1 1.1 fusion.1
  9.2 1.4 broadcast_in_dim.2
  10.6 1.6 reshape.21
  12.3 0.0 copy-done
  12.3 0.0 copy-done.1
  12.3 1.5 fusion
  13.8 2.1 copy.10
  15.9 0.0 reduce-scatter.4.cloned.1.call-update
  15.9 0.0 all-reduce.3.cloned.1.call-start
  16.0 4.0 convolution_multiply_fusion
  20.0 0.0 copy-start.2
  20.0 0.0 all-reduce.3.cloned.1.call-update
  20.0 1.3 dynamic-slice
  22.0 0.0 copy-done.2
  22.0 1.6 convolution_convert_fusion
  23.6 22.0 %reduce-scatter.4.cloned.1.call-done = bf16[192,288]{1,0:T(8,128)(2,1)} async-done(((bf16[768,288]{1,0:T(8,128)(2,1)}), bf16[192,288]{1,0:T(8,128)(2,1)}) %reduce-scatter.4.cloned.1.call-update) | async-done | bytes 110608
  45.6 1.7 copy.11
  47.3 1337.2 %all-reduce.3.cloned.1.call-done = f32[768,1152]{1,0:T(8,128)} async-done(((f32[768,1152]{1,0:T(8,128)}), f32[768,1152]{1,0:T(8,128)}) %all-reduce.3.cloned.1.call-update) | async-done | bytes 3538960
  1384.4 1.5 constant_dynamic-slice_fusion
  (1 shorter events, 0.0 us)
Async XLA Ops:
  8.0 4.3 copy-start
  8.0 37.6 %reduce-scatter.4.cloned.1.call-start = ((), (), s32[]{:S(2)}) async-start(), calls=%async_computation.1 | async-start | bytes 737280
  8.1 4.2 copy-start.1
  15.9 1368.5 %all-reduce.3.cloned.1.call-start = ((), (), s32[]{:S(2)}) async-start(), calls=%async_computation.2 | async-start | bytes 7077888
  20.0 2.0 copy-start.2
Sparse Core Ops, SparseCore 0:
  16.0 29.5 reduce-scatter.3
Sparse Core Ops, SparseCore 1:
  20.1 1364.3 all-reduce.2
where the time goes:
time: 1390 us
  waiting for transfers between devices  1360 us (98%)
  between operations  16.2 us (1%)
    unnamed x4, waiting for transfers between devices  1360 us
  transfers between devices with their start and end apart: 2, of which 2 were waited for; matrix products, arithmetic and copies ran while one was open for 1% of the time, Pallas kernels for 0%

commit v1 on v0

v1 whole, which is shorter than its diff:
```python
import functools

import jax
import jax.numpy as jnp
from jax import lax
from jax.experimental import pallas as pl
from jax.experimental.pallas import tpu as pltpu
from jax.sharding import PartitionSpec as P

TW = 96
NY, NX, NZ = 2, 4, 16
NREP = 4
OWN = 6
PAD = 8
MESH = pl.DeviceIdType.MESH
PARTS = (
    (0, 384, "y,x"),
    (384, 256, "x,y"),
    (640, 256, "x,y"),
    (896, 256, "xy"),
)


def div3(value, shift):
    return ((value >> shift) * 21846) >> 16


def kernel(amp_h, lam_h, int_h, pm_h, lad_o, ll_o, den_o, *scratch):
    (amp, lam, ints, pmap, ampt, lad, lpart, lrecv, lsem, ssem, rsem), bufs = scratch[:11], scratch[11:]
    pidx, rep = lax.axis_index("pair"), lax.axis_index("rep")
    z, x, y = lax.rem(pidx, NZ), lax.rem(pidx // NZ, NX), pidx // (NZ * NX)
    loads = [
        pltpu.make_async_copy(src, dst, lsem.at[k])
        for k, (src, dst) in enumerate(((pm_h, pmap), (amp_h, amp), (lam_h, lam), (int_h, ints)))
    ]
    for load in loads:
        load.start()

    def at(yy, xx, zz):
        return ((yy * NX + xx) * NZ + zz, rep)

    def xs(d):
        return lax.rem(x + d, NX)

    def zs(d):
        return lax.rem(z + d, NZ)

    offsets = [(dy, dx) for dx in (2, 1, 3, 0) for dy in (1, 0) if (dy, dx) != (0, 0)]
    zorder = (8, 7, 9, 6, 10, 5, 11, 4, 12, 3, 13, 2, 14, 1, 15)
    partners = [at(lax.rem(y + dy, NY), xs(dx), z) for dy, dx in offsets]
    partners += [at(y, x, zs(d)) for d in zorder]
    partners += [(pidx, lax.rem(rep + d, NREP)) for d in (1, 2, 3)]
    barrier = pltpu.get_barrier_semaphore()
    for device in partners:
        pl.semaphore_signal(barrier, inc=1, device_id=device, device_id_type=MESH)

    count = [0]

    def send(src, dst, device):
        k = count[0]
        count[0] += 1
        copy = pltpu.make_async_remote_copy(
            src_ref=src, dst_ref=dst, send_sem=ssem.at[k], recv_sem=rsem.at[k],
            device_id=device, device_id_type=MESH,
        )
        copy.start()
        return copy

    rows = amp.shape[0]
    f32, bf16 = jnp.float32, jnp.bfloat16

    def iota(shape, dim):
        return lax.broadcasted_iota(jnp.int32, shape, dim)

    tiles = rows // TW
    kt = pmap.shape[1]
    loads[0].wait()
    sel = (iota((rows, pmap.shape[0]), 1) == tiles * pidx + div3(iota((rows, pmap.shape[0]), 0), 5)).astype(f32)
    mask8 = jnp.dot(sel, pmap[...].astype(f32), preferred_element_type=f32)

    def mask_of(first, width):
        spread = (div3(first + iota((kt, width), 1), 5) == iota((kt, width), 0)).astype(f32)
        return jnp.dot(mask8, spread, preferred_element_type=f32)

    kw = amp.shape[1]
    live_mask = mask_of(0, kw).astype(bf16)
    eye = (iota((kw, kw), 0) == iota((kw, kw), 1)).astype(bf16)
    loads[1].wait()
    amp[...] = amp[...] * live_mask
    ampt[...] = lax.dot_general(
        eye, amp[...], (((1,), (1,)), ((), ())), preferred_element_type=f32
    ).astype(bf16)
    loads[2].wait()

    half = kw // NY
    first = []
    for n, (c0, width, order) in enumerate(PARTS):
        d, r1, s1, r2, e, r3 = bufs[6 * n : 6 * n + 6]
        for yy in range(NY):
            block = jnp.dot(
                ampt[yy * half : (yy + 1) * half, :], lam[:, c0 : c0 + width],
                preferred_element_type=f32,
            ).astype(bf16)
            for xx in range(NX):
                piece = block[xx * TW : (xx + 1) * TW, :]
                if order == "x,y":
                    d[xx, yy] = piece
                else:
                    d[yy, xx] = piece
        if n == 0:
            pl.semaphore_wait(barrier, len(partners))
        if order == "x,y":
            first.append([send(d.at[xs(k)], r1.at[k - 1], at(y, xs(k), z)) for k in (2, 1, 3)])
        elif order == "y,x":
            first.append([send(d.at[1 - y], r1.at[0], at(1 - y, x, z))])
        else:
            first.append([
                send(d.at[lax.rem(y + dy, NY), xs(dx)], r1.at[k], at(lax.rem(y + dy, NY), xs(dx), z))
                for k, (dy, dx) in enumerate(offsets)
            ])

    loads[3].wait()
    wide = kw // NREP
    for r in range(NREP):
        part = lax.dot_general(
            lam[...], ints[r * wide : (r + 1) * wide, :], (((1,), (1,)), ((), ())),
            preferred_element_type=f32,
        )
        lpart[r] = (part * mask_of(r * wide, wide)).astype(bf16)
    lam_sends = [
        send(lpart.at[lax.rem(rep + k, NREP)], lrecv.at[k - 1], (pidx, lax.rem(rep + k, NREP)))
        for k in (1, 2, 3)
    ]
    ncol = lam.shape[1]
    for c0 in range(0, ncol, 384):
        lad[:, c0 : c0 + 384] = jnp.dot(
            amp[...], ints[:, c0 : c0 + 384], preferred_element_type=f32
        ).astype(bf16)
    lad_copy = pltpu.make_async_copy(lad, lad_o, lsem.at[4])
    lad_copy.start()

    spread_rows = iota((NZ * PAD, TW), 0)
    spread = (
        ((spread_rows >> 3) * OWN + (spread_rows & 7) == iota((NZ * PAD, TW), 1))
        & ((spread_rows & 7) < OWN)
    ).astype(bf16)

    def to_z(n, total):
        c0, width, order = PARTS[n]
        e, r3 = bufs[6 * n + 4 : 6 * n + 6]
        padded = jnp.dot(spread, total.astype(bf16), preferred_element_type=f32)
        e[...] = padded.reshape(NZ, PAD, width).astype(bf16)
        return [send(e.at[zs(k)], r3.at[k - 1], at(y, x, zs(k))) for k in zorder]

    second, third = {}, {}

    def stage_one(n):
        c0, width, order = PARTS[n]
        d, r1, s1, r2, e, r3 = bufs[6 * n : 6 * n + 6]
        for copy in first[n]:
            copy.wait()
        if order == "x,y":
            total = d[x].astype(f32) + r1[0].astype(f32) + r1[1].astype(f32) + r1[2].astype(f32)
            s1[...] = total.astype(bf16)
            second[n] = [send(s1.at[1 - y], r2.at[0], at(1 - y, x, z))]
        elif order == "y,x":
            s1[...] = (d[y].astype(f32) + r1[0].astype(f32)).astype(bf16)
            second[n] = [send(s1.at[xs(k)], r2.at[k - 1], at(y, xs(k), z)) for k in (2, 1, 3)]
        else:
            total = d[y, x].astype(f32)
            for k in range(len(offsets)):
                total += r1[k].astype(f32)
            third[n] = to_z(n, total)

    def stage_two(n):
        c0, width, order = PARTS[n]
        d, r1, s1, r2, e, r3 = bufs[6 * n : 6 * n + 6]
        if n not in second:
            return
        for copy in second[n]:
            copy.wait()
        if order == "x,y":
            total = s1[y].astype(f32) + r2[0].astype(f32)
        else:
            total = s1[x].astype(f32) + r2[0].astype(f32) + r2[1].astype(f32) + r2[2].astype(f32)
        third[n] = to_z(n, total)

    stage_one(0)
    stage_one(1)
    for n in range(2, len(PARTS)):
        stage_one(n)
        stage_two(n - 2)
    stage_two(len(PARTS) - 2)
    stage_two(len(PARTS) - 1)

    for copy in lam_sends:
        copy.wait()
    total = lpart[rep].astype(f32)
    for k in range(3):
        total += lrecv[k].astype(f32)
    ll_o[...] = total.astype(bf16)

    factor = 1.0 / (rows * NY * NX * NZ) ** 0.5
    for n, (c0, width, order) in enumerate(PARTS):
        e, r3 = bufs[6 * n + 4 : 6 * n + 6]
        for copy in third[n]:
            copy.wait()
        total = e[z].astype(f32)
        for k in range(NZ - 1):
            total += r3[k].astype(f32)
        den_o[:, c0 : c0 + width] = total * factor
    lad_copy.wait()


def body(amplitudes, lambda_amps, integrals, pair_map):
    rows, kw = amplitudes.shape
    ncol = lambda_amps.shape[1]
    wide = kw // NREP
    bf16 = jnp.bfloat16
    scratch = [
        pltpu.VMEM((rows, kw), bf16),
        pltpu.VMEM((rows, ncol), bf16),
        pltpu.VMEM((kw, ncol), bf16),
        pltpu.VMEM(pair_map.shape, jnp.int32),
        pltpu.VMEM((kw, rows), bf16),
        pltpu.VMEM((rows, ncol), bf16),
        pltpu.VMEM((NREP, rows, wide), bf16),
        pltpu.VMEM((NREP - 1, rows, wide), bf16),
    ]
    sends = 3
    parts = []
    for _, width, order in PARTS:
        if order == "x,y":
            shapes = [(NX, NY, TW), (NX - 1, NY, TW), (NY, TW), (1, TW)]
            sends += NX
        elif order == "y,x":
            shapes = [(NY, NX, TW), (1, NX, TW), (NX, TW), (NX - 1, TW)]
            sends += NX
        else:
            shapes = [(NY, NX, TW), (NX * NY - 1, TW), (16,), (16,)]
            sends += NX * NY - 1
        shapes += [(NZ, PAD), (NZ - 1, PAD)]
        sends += NZ - 1
        parts += [pltpu.VMEM(shape + (width,), bf16) for shape in shapes]
    scratch += [
        pltpu.SemaphoreType.DMA((5,)),
        pltpu.SemaphoreType.DMA((sends,)),
        pltpu.SemaphoreType.DMA((sends,)),
    ]
    anywhere = pl.BlockSpec(memory_space=pl.ANY)
    vmem = pl.BlockSpec(memory_space=pltpu.VMEM)
    ladder, summed, density = pl.pallas_call(
        kernel,
        out_shape=(
            jax.ShapeDtypeStruct((rows, ncol), bf16),
            jax.ShapeDtypeStruct((rows, wide), bf16),
            jax.ShapeDtypeStruct((PAD, ncol), jnp.float32),
        ),
        in_specs=[anywhere] * 4,
        out_specs=(anywhere, vmem, vmem),
        scratch_shapes=scratch + parts,
        compiler_params=pltpu.CompilerParams(
            collective_id=0, has_side_effects=True, vmem_limit_bytes=56 * 2**20
        ),
        cost_estimate=pl.CostEstimate(
            flops=6 * rows * kw * ncol, bytes_accessed=4 * 2**20, transcendentals=0
        ),
    )(amplitudes, lambda_amps, integrals, pair_map)
    return ladder, summed, density[:OWN]


def solution(mesh):
    in_specs = (P("pair", None), P("pair", "rep"), P(None, "rep"), P())
    out_specs = (P("pair", "rep"), P("pair", "rep"), P("pair", "rep"))
    return jax.shard_map(body, mesh=mesh, in_specs=in_specs, out_specs=out_specs, check_vma=False)
```

time: 1390 us -> 59.6 us (0.04)
  waiting for transfers between devices: 1360 us -> 0 us
  Pallas kernels: 0 us -> 52.1 us
  between operations: 16.2 us -> 0.64 us
    unnamed x4 -> x0, waiting for transfers between devices: 1360 us -> none
    pallas_call x0 -> x1, Pallas kernels: none -> 52.1 us  [body(): pl.pallas_call(kernel, out_shape=(jax.ShapeDtypeStruct((rows, ncol), bf16...]
  transfers between devices with their start and end apart: 2 -> 0, of which waited for: 2 -> 0; matrix products, arithmetic and copies ran while one was open for 1% -> 0% of each run, Pallas kernels for 0% -> 0%
where the time goes in v1:
time: 59.6 us; the launch traced here: 59.2 us
  Pallas kernels  52.1 us (87%)
  local copies, waits for them, and re-layouts  6.46 us (11%)
  between operations  0.64 us (1%)
    pallas_call x1, Pallas kernels, body(): pl.pallas_call(kernel, out_shape=(jax.ShapeDtypeStruct((rows, ncol), bf16...  52.1 us
    unnamed x4, local copies, waits for them, and re-layouts  6.46 us

profile of v1, /device:TPU:24, one launch (start us, length us, event | category | flops | bytes accessed | tf_op | source)
XLA Modules:
  0.0 59.2 jit_solution(8546380539845482140)
XLA Ops:
  0.6 1.5 %copy.7.pm_h = s32[384,8]{1,0:T(8,128)} copy(s32[384,8]{0,1:T(8,128)} %param.7) | data formatting | bytes 24576 | tf_op args[3]
  2.1 52.1 %shard_map.67 = (bf16[288,1152]{1,0:T(8,128)(2,1)}, bf16[288,192]{1,0:T(8,128)(2,1)}, f32[8,1152]{1,0:T(8,128)}) custom-call(bf16[288,768]{1,0:T(8,128)(2,1)} %amp_h.1, bf16[288,1152]{1,0:T(8,128)(2,1)} %lam_h.1, bf16[768,1152]{1,0:T(8,128)(2,1)} %int_h.1, s32[384,8]{1,0:T(8,128)} %copy.7.pm_h), custom_call_target="tpu_custom_call" | custom-call | flops 1528823808 | bytes 4194304 | tf_op jit(solution)/shard_map/pallas_call | solution.py:252
  54.3 2.0 %copy.11 = bf16[288,1152]{1,0:T(8,128)(2,1)} copy(bf16[288,1152]{1,0:T(8,128)(2,1)} %get-tuple-element.12) | data formatting | bytes 1327104
  56.3 1.6 %copy.12 = bf16[288,192]{1,0:T(8,128)(2,1)} copy(bf16[288,192]{1,0:T(8,128)(2,1)} %get-tuple-element.13) | data formatting | bytes 221184
  57.8 1.4 %copy.13 = f32[6,1152]{1,0:T(8,128)} copy(f32[6,1152]{1,0:T(8,128)} %bitcast.1) | data formatting | bytes 55296

commit v2 on v1

v2 whole, which is shorter than its diff:
```python
import math

import jax
import jax.numpy as jnp
from jax import lax
from jax.experimental import pallas as pl
from jax.experimental.pallas import tpu as pltpu
from jax.sharding import PartitionSpec as P

TW = 96
NY, NX, NZ = 2, 4, 16
NREP = 4
OWN = 6
PAD = 8
MESH = pl.DeviceIdType.MESH
PARTS = (
    (0, 256, ("x", "y")),
    (256, 256, ("yx",)),
    (512, 256, ("p0", "x", "y")),
    (768, 384, ("p1", "yx")),
)
ORDER = ((0, 0), (2, 0), (3, 0), (1, 0), (0, 1), (2, 1), (3, 1), (2, 2))
CLOSE = (0, 1, 3, 2)


def axes_of(steps):
    sizes = {"x": (NX,), "y": (NY,), "yx": (NY, NX), "p0": (2,), "p1": (2,)}
    paired = "p0" in steps or "p1" in steps
    return [sizes[step] for step in steps], TW // 2 if paired else TW, NZ // 2 if paired else NZ


def div3(value, shift):
    return ((value >> shift) * 21846) >> 16


def kernel(amp_h, lam_h, int_h, pm_h, lad_o, ll_o, den_o, *scratch):
    (amp, lam, ints, pmap, ampt, ampp, lad, lpart, lrecv, lsem, ssem, rsem), bufs = scratch[:12], list(scratch[12:])
    pidx, rep = lax.axis_index("pair"), lax.axis_index("rep")
    z, x, y = lax.rem(pidx, NZ), lax.rem(pidx // NZ, NX), pidx // (NZ * NX)
    loads = [
        pltpu.make_async_copy(src, dst, lsem.at[k])
        for k, (src, dst) in enumerate(((pm_h, pmap), (amp_h, amp), (lam_h, lam), (int_h, ints)))
    ]
    for load in loads:
        load.start()

    def at(yy, xx, zz):
        return ((yy * NX + xx) * NZ + zz, rep)

    def xs(d):
        return lax.rem(x + d, NX)

    def zs(d):
        return lax.rem(z + d, NZ)

    offsets = [(dy, dx) for dx in (2, 1, 3, 0) for dy in (1, 0) if (dy, dx) != (0, 0)]
    zorder = (8, 7, 9, 6, 10, 5, 11, 4, 12, 3, 13, 2, 14, 1, 15)
    partners = [at(lax.rem(y + dy, NY), xs(dx), z) for dy, dx in offsets]
    partners += [at(y, x, zs(d)) for d in zorder]
    partners += [(pidx, lax.rem(rep + d, NREP)) for d in (1, 2, 3)]
    barrier = pltpu.get_barrier_semaphore()
    for device in partners:
        pl.semaphore_signal(barrier, inc=1, device_id=device, device_id_type=MESH)

    count = [0]

    def send(src, dst, device):
        k = count[0]
        count[0] += 1
        copy = pltpu.make_async_remote_copy(
            src_ref=src, dst_ref=dst, send_sem=ssem.at[k], recv_sem=rsem.at[k],
            device_id=device, device_id_type=MESH,
        )
        copy.start()
        return copy

    rows = amp.shape[0]
    f32, bf16 = jnp.float32, jnp.bfloat16

    def iota(shape, dim):
        return lax.broadcasted_iota(jnp.int32, shape, dim)

    tiles = rows // TW
    kt, ntiles = pmap.shape
    loads[0].wait()
    sel = (iota((rows, ntiles), 1) == tiles * pidx + div3(iota((rows, ntiles), 0), 5)).astype(f32)
    mask8 = lax.dot_general(
        sel, pmap[...].astype(f32), (((1,), (1,)), ((), ())), preferred_element_type=f32
    )

    def mask_of(first, width):
        spread = (div3(first + iota((kt, width), 1), 5) == iota((kt, width), 0)).astype(f32)
        return jnp.dot(mask8, spread, preferred_element_type=f32)

    kw = amp.shape[1]
    live_mask = mask_of(0, kw).astype(bf16)
    lanes, turned = iota((kw, kw), 1), iota((kw, 1), 0)
    eye = (turned == lanes).astype(bf16)
    odd = (turned >= kw // 2).astype(jnp.int32)
    inner = turned - odd * (kw // 2)
    sixth = div3(inner, 1)
    by_parity = (2 * OWN * sixth + OWN * odd + inner - OWN * sixth == lanes).astype(bf16)
    loads[1].wait()
    amp[...] = amp[...] * live_mask
    for order, dst in ((by_parity, ampp), (eye, ampt)):
        dst[...] = lax.dot_general(
            order, amp[...], (((1,), (1,)), ((), ())), preferred_element_type=f32
        ).astype(bf16)
    loads[2].wait()

    half = kw // 2
    zb = lax.rem(z, 2)
    mine = {"x": (x,), "y": (y,), "yx": (y, x), "p0": (zb,), "p1": (zb,)}
    peers = {
        "x": [((xs(k),), at(y, xs(k), z)) for k in (2, 1, 3)],
        "y": [((1 - y,), at(1 - y, x, z))],
        "yx": [
            ((lax.rem(y + dy, NY), xs(dx)), at(lax.rem(y + dy, NY), xs(dx), z)) for dy, dx in offsets
        ],
        "p0": [((1 - zb,), at(y, x, zs(NZ + 1 - 2 * zb)))],
        "p1": [((1 - zb,), at(y, x, zs(NZ - 1 + 2 * zb)))],
    }
    cur, recv, last, flying = [], [], [], []
    for c0, width, steps in PARTS:
        cur.append([bufs.pop(0) for _ in steps])
        recv.append([bufs.pop(0) for _ in steps])
        last.append((bufs.pop(0), bufs.pop(0)))
        flying.append(None)

    def launch(n, s):
        flying[n] = [
            send(cur[n][s].at[block], recv[n][s].at[k], device)
            for k, (block, device) in enumerate(peers[PARTS[n][2][s]])
        ]

    for n, (c0, width, steps) in enumerate(PARTS):
        axes, deep, members = axes_of(steps)
        paired = deep < TW
        for hi in range(2):
            block = jnp.dot(
                (ampp if paired else ampt)[hi * half : (hi + 1) * half, :], lam[:, c0 : c0 + width],
                preferred_element_type=f32,
            ).astype(bf16)
            for lo in range(half // deep):
                index = {"x": (lo % NX,), "p0": (hi,), "p1": (hi,)}
                index["y"] = (lo // NX if paired else hi,)
                index["yx"] = index["y"] + index["x"]
                where = sum((index[step] for step in steps), ())
                cur[n][0][where] = block[lo * deep : (lo + 1) * deep, :]
        if n == 0:
            pl.semaphore_wait(barrier, len(partners))
        launch(n, 0)

    loads[3].wait()
    wide = kw // NREP
    for r in range(NREP):
        part = lax.dot_general(
            lam[...], ints[r * wide : (r + 1) * wide, :], (((1,), (1,)), ((), ())),
            preferred_element_type=f32,
        )
        lpart[r] = (part * mask_of(r * wide, wide)).astype(bf16)
    lam_sends = [
        send(lpart.at[lax.rem(rep + k, NREP)], lrecv.at[k - 1], (pidx, lax.rem(rep + k, NREP)))
        for k in (1, 2, 3)
    ]
    ncol = lam.shape[1]
    for c0 in range(0, ncol, 384):
        lad[:, c0 : c0 + 384] = jnp.dot(
            amp[...], ints[:, c0 : c0 + 384], preferred_element_type=f32
        ).astype(bf16)
    lad_copy = pltpu.make_async_copy(lad, lad_o, lsem.at[4])
    lad_copy.start()

    def spread_of(members):
        spread_rows = iota((members * PAD, 1), 0)
        slot = spread_rows & (PAD - 1)
        source = jnp.where(slot < OWN, (spread_rows >> 3) * OWN + slot, -1)
        return (source == iota((members * PAD, members * OWN), 1)).astype(bf16)

    def finish_step(n, s):
        c0, width, steps = PARTS[n]
        axes, deep, members = axes_of(steps)
        for copy in flying[n]:
            copy.wait()
        total = cur[n][s][mine[steps[s]]].astype(f32)
        for k in range(len(flying[n])):
            total += recv[n][s][k].astype(f32)
        if s + 1 < len(steps):
            cur[n][s + 1][...] = total.astype(bf16)
            launch(n, s + 1)
            return
        out, into = last[n]
        padded = jnp.dot(spread_of(members), total.astype(bf16), preferred_element_type=f32)
        out[...] = padded.reshape(members, PAD, width).astype(bf16)
        step = NZ // members
        place = z // step
        flying[n] = [
            send(out.at[lax.rem(place + k, members)], into.at[k - 1], at(y, x, zs(k * step)))
            for k in sorted(range(1, members), key=lambda k: -min(k, members - k))
        ]

    for n, s in ORDER:
        finish_step(n, s)

    for copy in lam_sends:
        copy.wait()
    total = lpart[rep].astype(f32)
    for k in range(3):
        total += lrecv[k].astype(f32)
    ll_o[...] = total.astype(bf16)

    factor = 1.0 / (rows * NY * NX * NZ) ** 0.5
    for n in CLOSE:
        c0, width, steps = PARTS[n]
        out, into = last[n]
        members = out.shape[0]
        for copy in flying[n]:
            copy.wait()
        total = out[z // (NZ // members)].astype(f32)
        for k in range(members - 1):
            total += into[k].astype(f32)
        den_o[:, c0 : c0 + width] = total * factor
    lad_copy.wait()


def finish(lad_i, ll_i, den_i, lad_o, ll_o, den_o):
    lad_o[...] = lad_i[...]
    ll_o[...] = ll_i[...]
    den_o[...] = den_i[:OWN, :]


def body(amplitudes, lambda_amps, integrals, pair_map):
    rows, kw = amplitudes.shape
    ncol = lambda_amps.shape[1]
    wide = kw // NREP
    bf16 = jnp.bfloat16
    scratch = [
        pltpu.VMEM((rows, kw), bf16),
        pltpu.VMEM((rows, ncol), bf16),
        pltpu.VMEM((kw, ncol), bf16),
        pltpu.VMEM(pair_map.shape[::-1], jnp.int32),
        pltpu.VMEM((kw, rows), bf16),
        pltpu.VMEM((kw, rows), bf16),
        pltpu.VMEM((rows, ncol), bf16),
        pltpu.VMEM((NREP, rows, wide), bf16),
        pltpu.VMEM((NREP - 1, rows, wide), bf16),
    ]
    sends = 3
    parts = []
    for _, width, steps in PARTS:
        axes, deep, members = axes_of(steps)
        dims = [sum(axes[s:], ()) + (deep,) for s in range(len(steps))]
        shapes = dims + [
            (math.prod(axes[s]) - 1,) + sum(axes[s + 1 :], ()) + (deep,) for s in range(len(steps))
        ]
        sends += sum(math.prod(axis) - 1 for axis in axes) + members - 1
        shapes += [(members, PAD), (members - 1, PAD)]
        parts += [pltpu.VMEM(shape + (width,), bf16) for shape in shapes]
    scratch += [
        pltpu.SemaphoreType.DMA((5,)),
        pltpu.SemaphoreType.DMA((sends,)),
        pltpu.SemaphoreType.DMA((sends,)),
    ]
    anywhere = pl.BlockSpec(memory_space=pl.ANY)
    vmem = pl.BlockSpec(memory_space=pltpu.VMEM)
    ladder, summed, density = pl.pallas_call(
        kernel,
        out_shape=(
            jax.ShapeDtypeStruct((rows, ncol), bf16),
            jax.ShapeDtypeStruct((rows, wide), bf16),
            jax.ShapeDtypeStruct((PAD, ncol), jnp.float32),
        ),
        in_specs=[anywhere] * 4,
        out_specs=(anywhere, vmem, vmem),
        scratch_shapes=scratch + parts,
        compiler_params=pltpu.CompilerParams(
            collective_id=0, has_side_effects=True, vmem_limit_bytes=56 * 2**20
        ),
        cost_estimate=pl.CostEstimate(
            flops=6 * rows * kw * ncol, bytes_accessed=4 * 2**20, transcendentals=0
        ),
    )(amplitudes, lambda_amps, integrals, pair_map.T)
    return pl.pallas_call(
        finish,
        out_shape=(
            jax.ShapeDtypeStruct((rows, ncol), bf16),
            jax.ShapeDtypeStruct((rows, wide), bf16),
            jax.ShapeDtypeStruct((OWN, ncol), jnp.float32),
        ),
        in_specs=[vmem] * 3,
        out_specs=(vmem,) * 3,
    )(ladder, summed, density)


def solution(mesh):
    in_specs = (P("pair", None), P("pair", "rep"), P(None, "rep"), P())
    out_specs = (P("pair", "rep"), P("pair", "rep"), P("pair", "rep"))
    return jax.shard_map(body, mesh=mesh, in_specs=in_specs, out_specs=out_specs, check_vma=False)
```

time: 59.6 us -> 48.1 us (0.81)
  the two profiles are of different devices: /device:TPU:24 before, /device:TPU:2 now
where the time goes in v2:
time: 48.1 us; the launch traced here: 47.9 us
  Pallas kernels  47.2 us (98%)
  between operations  0.64 us (1%)
    pallas_call x1, Pallas kernels, body(): pl.pallas_call(kernel, out_shape=(jax.ShapeDtypeStruct((rows, ncol), bf16...  45.2 us
    pallas_call x1, Pallas kernels, body(): pl.pallas_call(finish, out_shape=(jax.ShapeDtypeStruct((rows, ncol), bf16...  2.08 us

profile of v2, /device:TPU:2, one launch (start us, length us, event | category | flops | bytes accessed | tf_op | source)
XLA Modules:
  0.0 47.9 jit_solution(6917964321138912218)
XLA Ops:
  0.6 45.2 %shard_map.67 = (bf16[288,1152]{1,0:T(8,128)(2,1)}, bf16[288,192]{1,0:T(8,128)(2,1)}, f32[8,1152]{1,0:T(8,128)}) custom-call(bf16[288,768]{1,0:T(8,128)(2,1)} %amp_h.1, bf16[288,1152]{1,0:T(8,128)(2,1)} %lam_h.1, bf16[768,1152]{1,0:T(8,128)(2,1)} %int_h.1, s32[8,384]{1,0:T(8,128)} %bitcast.1), custom_call_target="tpu_custom_call" | custom-call | flops 1528823808 | bytes 4194304 | tf_op jit(solution)/shard_map/pallas_call | solution.py:266
  45.8 2.1 %shard_map.68 = (bf16[288,1152]{1,0:T(8,128)(2,1)}, bf16[288,192]{1,0:T(8,128)(2,1)}, f32[6,1152]{1,0:T(8,128)}) custom-call(bf16[288,1152]{1,0:T(8,128)(2,1)} %get-tuple-element.6.lad_i, bf16[288,192]{1,0:T(8,128)(2,1)} %get-tuple-element.7.ll_i, f32[8,1152]{1,0:T(8,128)} %get-tuple-element.8.den_i), custom_call_target="tpu_custom_call" | custom-call | tf_op jit(solution)/shard_map/pallas_call | solution.py:283

commit v3 on v2

--- a/solution.py
+++ b/solution.py
@@ -14,13 +14,18 @@
 PAD = 8
 MESH = pl.DeviceIdType.MESH
 PARTS = (
-    (0, 256, ("x", "y")),
+    (0, 256, ("p0", "yx")),
     (256, 256, ("yx",)),
-    (512, 256, ("p0", "x", "y")),
-    (768, 384, ("p1", "yx")),
+    (512, 128, ("yx",)),
+    (640, 128, ("p1", "yx")),
+    (768, 128, ("p1", "yx")),
+    (896, 128, ("p0", "yx")),
+    (1024, 128, ("p1", "yx")),
 )
-ORDER = ((0, 0), (2, 0), (3, 0), (1, 0), (0, 1), (2, 1), (3, 1), (2, 2))
-CLOSE = (0, 1, 3, 2)
+ORDER = ((3, 0), (0, 0), (4, 0), (5, 0), (1, 0), (6, 0), (2, 0), (3, 1), (0, 1), (4, 1), (5, 1), (6, 1))
+CLOSE = (1, 2, 3, 0, 4, 5, 6)
+START = (1, 2, 0, 3, 4, 5, 6)
+LAMBDA_AT = (2, 10)
 
 
 def axes_of(steps):
@@ -34,14 +39,14 @@
 
 
 def kernel(amp_h, lam_h, int_h, pm_h, lad_o, ll_o, den_o, *scratch):
-    (amp, lam, ints, pmap, ampt, ampp, lad, lpart, lrecv, lsem, ssem, rsem), bufs = scratch[:12], list(scratch[12:])
+    (amp, lam, ints, pmap, ampt, ampp, lad, lpart, lrecv, lsum, lfar, lsem, ssem, rsem, known), bufs = scratch[:15], list(scratch[15:])
     pidx, rep = lax.axis_index("pair"), lax.axis_index("rep")
     z, x, y = lax.rem(pidx, NZ), lax.rem(pidx // NZ, NX), pidx // (NZ * NX)
     loads = [
         pltpu.make_async_copy(src, dst, lsem.at[k])
         for k, (src, dst) in enumerate(((pm_h, pmap), (amp_h, amp), (lam_h, lam), (int_h, ints)))
     ]
-    for load in loads:
+    for load in loads[:3]:
         load.start()
 
     def at(yy, xx, zz):
@@ -54,13 +59,19 @@
         return lax.rem(z + d, NZ)
 
     offsets = [(dy, dx) for dx in (2, 1, 3, 0) for dy in (1, 0) if (dy, dx) != (0, 0)]
-    zorder = (8, 7, 9, 6, 10, 5, 11, 4, 12, 3, 13, 2, 14, 1, 15)
     partners = [at(lax.rem(y + dy, NY), xs(dx), z) for dy, dx in offsets]
-    partners += [at(y, x, zs(d)) for d in zorder]
-    partners += [(pidx, lax.rem(rep + d, NREP)) for d in (1, 2, 3)]
+    partners += [at(y, x, zs(d)) for d in (1, NZ - 1)]
+    core, ylo = lax.rem(rep, 2), rep // 2
+    partners += [(pidx, 2 * ylo + 1 - core), (pidx, 2 * (1 - ylo) + core)]
     barrier = pltpu.get_barrier_semaphore()
     for device in partners:
         pl.semaphore_signal(barrier, inc=1, device_id=device, device_id_type=MESH)
+
+    def greet(level):
+        for d in (2**level, NZ - 2**level):
+            pl.semaphore_signal(
+                known.at[level], inc=1, device_id=at(y, x, zs(d)), device_id_type=MESH
+            )
 
     count = [0]
 
@@ -83,30 +94,31 @@
     tiles = rows // TW
     kt, ntiles = pmap.shape
     loads[0].wait()
-    sel = (iota((rows, ntiles), 1) == tiles * pidx + div3(iota((rows, ntiles), 0), 5)).astype(f32)
+    sel = (iota((rows, ntiles), 1) == tiles * pidx + div3(iota((rows, ntiles), 0), 5)).astype(bf16)
     mask8 = lax.dot_general(
-        sel, pmap[...].astype(f32), (((1,), (1,)), ((), ())), preferred_element_type=f32
-    )
+        sel, pmap[...].astype(bf16), (((1,), (1,)), ((), ())), preferred_element_type=f32
+    ).astype(bf16)
 
     def mask_of(first, width):
-        spread = (div3(first + iota((kt, width), 1), 5) == iota((kt, width), 0)).astype(f32)
+        spread = (div3(first + iota((kt, width), 1), 5) == iota((kt, width), 0)).astype(bf16)
         return jnp.dot(mask8, spread, preferred_element_type=f32)
 
     kw = amp.shape[1]
     live_mask = mask_of(0, kw).astype(bf16)
-    lanes, turned = iota((kw, kw), 1), iota((kw, 1), 0)
-    eye = (turned == lanes).astype(bf16)
-    odd = (turned >= kw // 2).astype(jnp.int32)
-    inner = turned - odd * (kw // 2)
-    sixth = div3(inner, 1)
-    by_parity = (2 * OWN * sixth + OWN * odd + inner - OWN * sixth == lanes).astype(bf16)
+    blk = 256
+    eye = (iota((blk, 1), 0) == iota((blk, blk), 1)).astype(bf16)
     loads[1].wait()
     amp[...] = amp[...] * live_mask
-    for order, dst in ((by_parity, ampp), (eye, ampt)):
-        dst[...] = lax.dot_general(
-            order, amp[...], (((1,), (1,)), ((), ())), preferred_element_type=f32
+
+    def turn(order, columns):
+        return lax.dot_general(
+            order, amp[:, columns], (((1,), (1,)), ((), ())), preferred_element_type=f32
         ).astype(bf16)
+
+    for c0 in range(0, kw, blk):
+        ampt[c0 : c0 + blk, :] = turn(eye, slice(c0, c0 + blk))
     loads[2].wait()
+    loads[3].start()
 
     half = kw // 2
     zb = lax.rem(z, 2)
@@ -133,9 +145,25 @@
             for k, (block, device) in enumerate(peers[PARTS[n][2][s]])
         ]
 
-    for n, (c0, width, steps) in enumerate(PARTS):
+    def split_rows():
+        quarter = kw // 4
+        for hi in range(2):
+            for lo in range(2):
+                inner = iota((quarter, 1), 0)
+                sixth = div3(inner, 1)
+                source = 2 * OWN * sixth + OWN * hi + inner - OWN * sixth
+                order = (source == iota((quarter, half), 1)).astype(bf16)
+                r0 = hi * half + lo * quarter
+                ampp[r0 : r0 + quarter, :] = turn(order, slice(lo * half, lo * half + half))
+
+    split = False
+    for n in START:
+        c0, width, steps = PARTS[n]
         axes, deep, members = axes_of(steps)
         paired = deep < TW
+        if paired and not split:
+            split_rows()
+            split = True
         for hi in range(2):
             block = jnp.dot(
                 (ampp if paired else ampt)[hi * half : (hi + 1) * half, :], lam[:, c0 : c0 + width],
@@ -147,10 +175,13 @@
                 index["yx"] = index["y"] + index["x"]
                 where = sum((index[step] for step in steps), ())
                 cur[n][0][where] = block[lo * deep : (lo + 1) * deep, :]
-        if n == 0:
+        if n == START[0]:
             pl.semaphore_wait(barrier, len(partners))
+            greet(0)
         launch(n, 0)
 
+    pl.semaphore_wait(known.at[0], 2)
+    greet(1)
     loads[3].wait()
     wide = kw // NREP
     for r in range(NREP):
@@ -158,11 +189,10 @@
             lam[...], ints[r * wide : (r + 1) * wide, :], (((1,), (1,)), ((), ())),
             preferred_element_type=f32,
         )
-        lpart[r] = (part * mask_of(r * wide, wide)).astype(bf16)
-    lam_sends = [
-        send(lpart.at[lax.rem(rep + k, NREP)], lrecv.at[k - 1], (pidx, lax.rem(rep + k, NREP)))
-        for k in (1, 2, 3)
-    ]
+        lpart[r % 2, r // 2] = (part * mask_of(r * wide, wide)).astype(bf16)
+    over_core = send(lpart.at[1 - core], lrecv, (pidx, 2 * ylo + 1 - core))
+    pl.semaphore_wait(known.at[1], 2)
+    greet(2)
     ncol = lam.shape[1]
     for c0 in range(0, ncol, 384):
         lad[:, c0 : c0 + 384] = jnp.dot(
@@ -170,6 +200,8 @@
         ).astype(bf16)
     lad_copy = pltpu.make_async_copy(lad, lad_o, lsem.at[4])
     lad_copy.start()
+
+    pl.semaphore_wait(known.at[2], 2)
 
     def spread_of(members):
         spread_rows = iota((members * PAD, 1), 0)
@@ -199,15 +231,16 @@
             for k in sorted(range(1, members), key=lambda k: -min(k, members - k))
         ]
 
-    for n, s in ORDER:
+    for k, (n, s) in enumerate(ORDER):
+        if k == LAMBDA_AT[0]:
+            over_core.wait()
+            lsum[...] = (lpart[core].astype(f32) + lrecv[...].astype(f32)).astype(bf16)
+        if k == LAMBDA_AT[1]:
+            over_y = send(lsum.at[1 - ylo], lfar, (pidx, 2 * (1 - ylo) + core))
         finish_step(n, s)
 
-    for copy in lam_sends:
-        copy.wait()
-    total = lpart[rep].astype(f32)
-    for k in range(3):
-        total += lrecv[k].astype(f32)
-    ll_o[...] = total.astype(bf16)
+    over_y.wait()
+    ll_o[...] = (lsum[ylo].astype(f32) + lfar[...].astype(f32)).astype(bf16)
 
     factor = 1.0 / (rows * NY * NX * NZ) ** 0.5
     for n in CLOSE:
@@ -242,10 +275,12 @@
         pltpu.VMEM((kw, rows), bf16),
         pltpu.VMEM((kw, rows), bf16),
         pltpu.VMEM((rows, ncol), bf16),
-        pltpu.VMEM((NREP, rows, wide), bf16),
-        pltpu.VMEM((NREP - 1, rows, wide), bf16),
+        pltpu.VMEM((2, NREP // 2, rows, wide), bf16),
+        pltpu.VMEM((NREP // 2, rows, wide), bf16),
+        pltpu.VMEM((NREP // 2, rows, wide), bf16),
+        pltpu.VMEM((rows, wide), bf16),
     ]
-    sends = 3
+    sends = 2
     parts = []
     for _, width, steps in PARTS:
         axes, deep, members = axes_of(steps)
@@ -260,6 +295,7 @@
         pltpu.SemaphoreType.DMA((5,)),
         pltpu.SemaphoreType.DMA((sends,)),
         pltpu.SemaphoreType.DMA((sends,)),
+        pltpu.SemaphoreType.REGULAR((3,)),
     ]
     anywhere = pl.BlockSpec(memory_space=pl.ANY)
     vmem = pl.BlockSpec(memory_space=pltpu.VMEM)

time: 48.1 us -> 42.5 us (0.88)
  the two profiles are of different devices: /device:TPU:2 before, /device:TPU:24 now
where the time goes in v3:
time: 42.5 us; the launch traced here: 42.2 us
  Pallas kernels  41.5 us (98%)
  between operations  0.64 us (2%)
    pallas_call x1, Pallas kernels, body(): pl.pallas_call(kernel, out_shape=(jax.ShapeDtypeStruct((rows, ncol), bf16...  39.4 us
    pallas_call x1, Pallas kernels, body(): pl.pallas_call(finish, out_shape=(jax.ShapeDtypeStruct((rows, ncol), bf16...  2.08 us

profile of v3, /device:TPU:24, one launch (start us, length us, event | category | flops | bytes accessed | tf_op | source)
XLA Modules:
  0.0 42.2 jit_solution(11270926994649322687)
XLA Ops:
  0.6 39.4 %shard_map.67 = (bf16[288,1152]{1,0:T(8,128)(2,1)}, bf16[288,192]{1,0:T(8,128)(2,1)}, f32[8,1152]{1,0:T(8,128)}) custom-call(bf16[288,768]{1,0:T(8,128)(2,1)} %amp_h.1, bf16[288,1152]{1,0:T(8,128)(2,1)} %lam_h.1, bf16[768,1152]{1,0:T(8,128)(2,1)} %int_h.1, s32[8,384]{1,0:T(8,128)} %bitcast.1), custom_call_target="tpu_custom_call" | custom-call | flops 1528823808 | bytes 4194304 | tf_op jit(solution)/shard_map/pallas_call | solution.py:302
  40.1 2.1 %shard_map.68 = (bf16[288,1152]{1,0:T(8,128)(2,1)}, bf16[288,192]{1,0:T(8,128)(2,1)}, f32[6,1152]{1,0:T(8,128)}) custom-call(bf16[288,1152]{1,0:T(8,128)(2,1)} %get-tuple-element.6.lad_i, bf16[288,192]{1,0:T(8,128)(2,1)} %get-tuple-element.7.ll_i, f32[8,1152]{1,0:T(8,128)} %get-tuple-element.8.den_i), custom_call_target="tpu_custom_call" | custom-call | tf_op jit(solution)/shard_map/pallas_call | solution.py:319

commit v4 on v3

--- a/solution.py
+++ b/solution.py
@@ -75,15 +75,19 @@
 
     count = [0]
 
-    def send(src, dst, device):
+    def send(blocks, into):
         k = count[0]
         count[0] += 1
-        copy = pltpu.make_async_remote_copy(
-            src_ref=src, dst_ref=dst, send_sem=ssem.at[k], recv_sem=rsem.at[k],
-            device_id=device, device_id_type=MESH,
-        )
-        copy.start()
-        return copy
+
+        def copy_of(src, dst, device):
+            return pltpu.make_async_remote_copy(
+                src_ref=src, dst_ref=dst, send_sem=ssem.at[k], recv_sem=rsem.at[k],
+                device_id=device, device_id_type=MESH,
+            )
+
+        for src, dst, device in blocks:
+            copy_of(src, dst, device).start()
+        return copy_of(into, into, blocks[0][2])
 
     rows = amp.shape[0]
     f32, bf16 = jnp.float32, jnp.bfloat16
@@ -132,7 +136,7 @@
         "p0": [((1 - zb,), at(y, x, zs(NZ + 1 - 2 * zb)))],
         "p1": [((1 - zb,), at(y, x, zs(NZ - 1 + 2 * zb)))],
     }
-    cur, recv, last, flying = [], [], [], []
+    cur, recv, last, flying, flown = [], [], [], [], []
     for c0, width, steps in PARTS:
         cur.append([bufs.pop(0) for _ in steps])
         recv.append([bufs.pop(0) for _ in steps])
@@ -140,10 +144,14 @@
         flying.append(None)
 
     def launch(n, s):
-        flying[n] = [
-            send(cur[n][s].at[block], recv[n][s].at[k], device)
-            for k, (block, device) in enumerate(peers[PARTS[n][2][s]])
-        ]
+        into = recv[n][s]
+        flying[n] = send(
+            [
+                (cur[n][s].at[block], into.at[k], device)
+                for k, (block, device) in enumerate(peers[PARTS[n][2][s]])
+            ],
+            into,
+        )
 
     def split_rows():
         quarter = kw // 4
@@ -190,7 +198,7 @@
             preferred_element_type=f32,
         )
         lpart[r % 2, r // 2] = (part * mask_of(r * wide, wide)).astype(bf16)
-    over_core = send(lpart.at[1 - core], lrecv, (pidx, 2 * ylo + 1 - core))
+    over_core = send([(lpart.at[1 - core], lrecv, (pidx, 2 * ylo + 1 - core))], lrecv)
     pl.semaphore_wait(known.at[1], 2)
     greet(2)
     ncol = lam.shape[1]
@@ -212,10 +220,10 @@
     def finish_step(n, s):
         c0, width, steps = PARTS[n]
         axes, deep, members = axes_of(steps)
-        for copy in flying[n]:
-            copy.wait()
+        flying[n].wait_recv()
+        flown.append(flying[n])
         total = cur[n][s][mine[steps[s]]].astype(f32)
-        for k in range(len(flying[n])):
+        for k in range(recv[n][s].shape[0]):
             total += recv[n][s][k].astype(f32)
         if s + 1 < len(steps):
             cur[n][s + 1][...] = total.astype(bf16)
@@ -223,23 +231,28 @@
             return
         out, into = last[n]
         padded = jnp.dot(spread_of(members), total.astype(bf16), preferred_element_type=f32)
-        out[...] = padded.reshape(members, PAD, width).astype(bf16)
+        out[...] = padded.reshape(members, PAD, width)[:, :OWN, :].astype(bf16)
         step = NZ // members
         place = z // step
-        flying[n] = [
-            send(out.at[lax.rem(place + k, members)], into.at[k - 1], at(y, x, zs(k * step)))
-            for k in sorted(range(1, members), key=lambda k: -min(k, members - k))
-        ]
+        flying[n] = send(
+            [
+                (out.at[lax.rem(place + k, members)], into.at[k - 1], at(y, x, zs(k * step)))
+                for k in sorted(range(1, members), key=lambda k: -min(k, members - k))
+            ],
+            into,
+        )
 
     for k, (n, s) in enumerate(ORDER):
         if k == LAMBDA_AT[0]:
             over_core.wait()
             lsum[...] = (lpart[core].astype(f32) + lrecv[...].astype(f32)).astype(bf16)
         if k == LAMBDA_AT[1]:
-            over_y = send(lsum.at[1 - ylo], lfar, (pidx, 2 * (1 - ylo) + core))
+            over_y = send([(lsum.at[1 - ylo], lfar, (pidx, 2 * (1 - ylo) + core))], lfar)
         finish_step(n, s)
 
     over_y.wait()
+    for copies in flown:
+        copies.wait_send()
     ll_o[...] = (lsum[ylo].astype(f32) + lfar[...].astype(f32)).astype(bf16)
 
     factor = 1.0 / (rows * NY * NX * NZ) ** 0.5
@@ -247,8 +260,7 @@
         c0, width, steps = PARTS[n]
         out, into = last[n]
         members = out.shape[0]
-        for copy in flying[n]:
-            copy.wait()
+        flying[n].wait()
         total = out[z // (NZ // members)].astype(f32)
         for k in range(members - 1):
             total += into[k].astype(f32)
@@ -259,7 +271,7 @@
 def finish(lad_i, ll_i, den_i, lad_o, ll_o, den_o):
     lad_o[...] = lad_i[...]
     ll_o[...] = ll_i[...]
-    den_o[...] = den_i[:OWN, :]
+    den_o[...] = den_i[...]
 
 
 def body(amplitudes, lambda_amps, integrals, pair_map):
@@ -288,8 +300,8 @@
         shapes = dims + [
             (math.prod(axes[s]) - 1,) + sum(axes[s + 1 :], ()) + (deep,) for s in range(len(steps))
         ]
-        sends += sum(math.prod(axis) - 1 for axis in axes) + members - 1
-        shapes += [(members, PAD), (members - 1, PAD)]
+        sends += len(steps) + 1
+        shapes += [(members, OWN), (members - 1, OWN)]
         parts += [pltpu.VMEM(shape + (width,), bf16) for shape in shapes]
     scratch += [
         pltpu.SemaphoreType.DMA((5,)),
@@ -304,7 +316,7 @@
         out_shape=(
             jax.ShapeDtypeStruct((rows, ncol), bf16),
             jax.ShapeDtypeStruct((rows, wide), bf16),
-            jax.ShapeDtypeStruct((PAD, ncol), jnp.float32),
+            jax.ShapeDtypeStruct((OWN, ncol), jnp.float32),
         ),
         in_specs=[anywhere] * 4,
         out_specs=(anywhere, vmem, vmem),

time: 42.5 us -> 40.6 us (0.955)
  Pallas kernels: 41.5 us -> 39.7 us
    pallas_call x1, Pallas kernels: 39.4 us -> 37.6 us  [body(): pl.pallas_call(kernel, out_shape=(jax.ShapeDtypeStruct((rows, ncol), bf16...]
where the time goes in v4:
time: 40.6 us; the launch traced here: 40.3 us
  Pallas kernels  39.7 us (98%)
  between operations  0.64 us (2%)
    pallas_call x1, Pallas kernels, body(): pl.pallas_call(kernel, out_shape=(jax.ShapeDtypeStruct((rows, ncol), bf16...  37.6 us
    pallas_call x1, Pallas kernels, body(): pl.pallas_call(finish, out_shape=(jax.ShapeDtypeStruct((rows, ncol), bf16...  2.08 us

profile of v4, /device:TPU:24, one launch (start us, length us, event | category | flops | bytes accessed | tf_op | source)
XLA Modules:
  0.0 40.3 jit_solution(5797993236355299325)
XLA Ops:
  0.6 37.6 %shard_map.67 = (bf16[288,1152]{1,0:T(8,128)(2,1)}, bf16[288,192]{1,0:T(8,128)(2,1)}, f32[6,1152]{1,0:T(8,128)}) custom-call(bf16[288,768]{1,0:T(8,128)(2,1)} %amp_h.1, bf16[288,1152]{1,0:T(8,128)(2,1)} %lam_h.1, bf16[768,1152]{1,0:T(8,128)(2,1)} %int_h.1, s32[8,384]{1,0:T(8,128)} %bitcast.1), custom_call_target="tpu_custom_call" | custom-call | flops 1528823808 | bytes 4194304 | tf_op jit(solution)/shard_map/pallas_call | solution.py:314
  38.2 2.1 %shard_map.68 = (bf16[288,1152]{1,0:T(8,128)(2,1)}, bf16[288,192]{1,0:T(8,128)(2,1)}, f32[6,1152]{1,0:T(8,128)}) custom-call(bf16[288,1152]{1,0:T(8,128)(2,1)} %get-tuple-element.6.lad_i, bf16[288,192]{1,0:T(8,128)(2,1)} %get-tuple-element.7.ll_i, f32[6,1152]{1,0:T(8,128)} %get-tuple-element.8.den_i), custom_call_target="tpu_custom_call" | custom-call | tf_op jit(solution)/shard_map/pallas_call | solution.py:331

commit v5 on v4

--- a/solution.py
+++ b/solution.py
@@ -15,17 +15,15 @@
 MESH = pl.DeviceIdType.MESH
 PARTS = (
     (0, 256, ("p0", "yx")),
-    (256, 256, ("yx",)),
-    (512, 128, ("yx",)),
-    (640, 128, ("p1", "yx")),
-    (768, 128, ("p1", "yx")),
+    (256, 384, ("yx",)),
+    (640, 256, ("p1", "yx")),
     (896, 128, ("p0", "yx")),
     (1024, 128, ("p1", "yx")),
 )
-ORDER = ((3, 0), (0, 0), (4, 0), (5, 0), (1, 0), (6, 0), (2, 0), (3, 1), (0, 1), (4, 1), (5, 1), (6, 1))
-CLOSE = (1, 2, 3, 0, 4, 5, 6)
-START = (1, 2, 0, 3, 4, 5, 6)
-LAMBDA_AT = (2, 10)
+ORDER = ((0, 0), (2, 0), (3, 0), (4, 0), (1, 0), (0, 1), (2, 1), (3, 1), (4, 1))
+CLOSE = (1, 0, 2, 3, 4)
+START = (1, 0, 2, 3, 4)
+LAMBDA_AT = (2, 7)
 
 
 def axes_of(steps):
@@ -201,14 +199,6 @@
     over_core = send([(lpart.at[1 - core], lrecv, (pidx, 2 * ylo + 1 - core))], lrecv)
     pl.semaphore_wait(known.at[1], 2)
     greet(2)
-    ncol = lam.shape[1]
-    for c0 in range(0, ncol, 384):
-        lad[:, c0 : c0 + 384] = jnp.dot(
-            amp[...], ints[:, c0 : c0 + 384], preferred_element_type=f32
-        ).astype(bf16)
-    lad_copy = pltpu.make_async_copy(lad, lad_o, lsem.at[4])
-    lad_copy.start()
-
     pl.semaphore_wait(known.at[2], 2)
 
     def spread_of(members):
@@ -249,6 +239,14 @@
         if k == LAMBDA_AT[1]:
             over_y = send([(lsum.at[1 - ylo], lfar, (pidx, 2 * (1 - ylo) + core))], lfar)
         finish_step(n, s)
+
+    ncol = lam.shape[1]
+    for c0 in range(0, ncol, 384):
+        lad[:, c0 : c0 + 384] = jnp.dot(
+            amp[...], ints[:, c0 : c0 + 384], preferred_element_type=f32
+        ).astype(bf16)
+    lad_copy = pltpu.make_async_copy(lad, lad_o, lsem.at[4])
+    lad_copy.start()
 
     over_y.wait()
     for copies in flown:

time: 40.6 us -> 40.1 us (0.988)
  no operation moved by 1% of the time
where the time goes in v5:
time: 40.1 us; the launch traced here: 40 us
  Pallas kernels  39.3 us (98%)
  between operations  0.64 us (2%)
    pallas_call x1, Pallas kernels, body(): pl.pallas_call(kernel, out_shape=(jax.ShapeDtypeStruct((rows, ncol), bf16...  37.2 us
    pallas_call x1, Pallas kernels, body(): pl.pallas_call(finish, out_shape=(jax.ShapeDtypeStruct((rows, ncol), bf16...  2.08 us

profile of v5, /device:TPU:24, one launch (start us, length us, event | category | flops | bytes accessed | tf_op | source)
XLA Modules:
  0.0 40.0 jit_solution(15122033755431163573)
XLA Ops:
  0.6 37.2 %shard_map.67 = (bf16[288,1152]{1,0:T(8,128)(2,1)}, bf16[288,192]{1,0:T(8,128)(2,1)}, f32[6,1152]{1,0:T(8,128)}) custom-call(bf16[288,768]{1,0:T(8,128)(2,1)} %amp_h.1, bf16[288,1152]{1,0:T(8,128)(2,1)} %lam_h.1, bf16[768,1152]{1,0:T(8,128)(2,1)} %int_h.1, s32[8,384]{1,0:T(8,128)} %bitcast.1), custom_call_target="tpu_custom_call" | custom-call | flops 1528823808 | bytes 4194304 | tf_op jit(solution)/shard_map/pallas_call | solution.py:312
  37.9 2.1 %shard_map.68 = (bf16[288,1152]{1,0:T(8,128)(2,1)}, bf16[288,192]{1,0:T(8,128)(2,1)}, f32[6,1152]{1,0:T(8,128)}) custom-call(bf16[288,1152]{1,0:T(8,128)(2,1)} %get-tuple-element.6.lad_i, bf16[288,192]{1,0:T(8,128)(2,1)} %get-tuple-element.7.ll_i, f32[6,1152]{1,0:T(8,128)} %get-tuple-element.8.den_i), custom_call_target="tpu_custom_call" | custom-call | tf_op jit(solution)/shard_map/pallas_call | solution.py:329
